TPU v7x, 32 devices: a whole 2x2x4 slice. The times are simulated.
32 devices in a mesh: chan: 8 (over z, core), seg: 4 (over y, x).
Axes of the slice: x: 2, y: 2, z: 4, core: 2. Of those that a mesh axis runs over, the one named last changes fastest.
Arguments:
- traces: float32 [16, 64, 7680], P('seg', None, 'chan'), may hold values from -40 to 40
- sources: int32 [64], replicated, may hold values from 0 to 63, as said below
- validity: int32 [16, 64], replicated, may hold values from 0 to 1, as said below
Outputs:
- correlation: float32 [64, 64, 512], P('seg', 'chan')
Inputs may be any that keep to these rules, and one draw needn't show every extreme that they name: `sources`: 64 distinct channel indices. `validity`: 1 marks a usable segment of a channel, 0 a discarded one; in every draw some channels are 0 in all segments.
All inputs are finite; a program needn't handle non-finite values.
Results may differ from a plain program's by a relative error of at most 0.0021.
Values may be sent and summed in bfloat16 or wider, within the bound.
No kernel may reach another device: no remote copies, remote signals or barrier semaphores. Data moves between devices by JAX's collectives and lax.ppermute only.
A program may use at most 128 MiB of HBM per device.

v0:
```python
import functools
import math

import jax
import jax.numpy as jnp
import ml_dtypes
import numpy as np
from jax import lax
from jax.experimental import pallas as pl
from jax.experimental.pallas import tpu as pltpu
from jax.sharding import PartitionSpec as P

LAGS = 512
BLOCK = 128
EPSILON = 1e-06
RADIX = 16
TABLE_ROWS = 24576
HALVES = 2
CHUNK = 640
STEPS = 32767.0
FINENESS = 64.0
VMEM_LIMIT = 50 * 1024 * 1024
SMALL_LIMIT = 16 * 1024 * 1024


def split_table(table):
    high = table.astype(ml_dtypes.bfloat16)
    low = (table - high.astype(np.float64)).astype(ml_dtypes.bfloat16)
    return high, low


def round_up(value, step):
    return -(-value // step) * step


def bin_order(bins_total):
    fine = bins_total // RADIX
    whole = fine // 128 * 128
    first = np.arange(RADIX)[:, None]
    head = (first + RADIX * np.arange(whole)[None, :]).reshape(-1)
    tail = (first + RADIX * np.arange(whole, fine)[None, :]).reshape(-1)
    return np.concatenate([head, tail])


def fourier_constants(length):
    span = length // RADIX
    span_pad = round_up(span, 128)
    fine = span // 2
    fine_pad = round_up(fine, 128)
    phase = 2.0 * np.pi / span * ((np.arange(span)[:, None] * np.arange(fine)[None, :]) % span)
    table = np.zeros((span_pad, 2 * fine_pad))
    table[:span, :fine] = np.cos(phase)
    table[:span, fine_pad : fine_pad + fine] = np.sin(phase)
    high, low = split_table(table)
    group = BLOCK // RADIX
    ids = np.arange(fine_pad) // group
    mean = ((ids[:, None] == ids[None, :]) / BLOCK).astype(ml_dtypes.bfloat16)
    return high, low, mean


def twists_of(length):
    span = length // RADIX
    turns = jnp.arange(RADIX, dtype=jnp.int32)[:, None] * jnp.arange(span, dtype=jnp.int32)[None, :]
    phase = (2.0 * math.pi / length) * turns.astype(jnp.float32)
    return jnp.concatenate([jnp.cos(phase), jnp.sin(phase)], axis=0)


@functools.cache
def all_tables(length):
    high, low, mean = fourier_constants(length)
    cos_table, sin_table, _ = lag_constants(length // 2)
    places = []
    pieces = []
    used = 0
    for table in (high, low, mean, cos_table, sin_table):
        columns = []
        for start in range(0, table.shape[1], LAGS // 2):
            columns.append(used)
            pieces.append(table[:, start : start + LAGS // 2])
            used += table.shape[0]
        places.append((columns, table.shape))
    pieces.append(np.zeros((max(0, TABLE_ROWS - used), LAGS // 2), ml_dtypes.bfloat16))
    return np.concatenate(pieces, axis=0), places


def table_copies(far, near, columns, arrivals, base):
    size = near.shape[0]
    return [
        pltpu.make_async_copy(
            far.at[pl.ds(row, size)],
            near.at[:, pl.ds(index * (LAGS // 2), LAGS // 2)],
            arrivals.at[base + index],
        )
        for index, row in enumerate(columns)
    ]


def lag_constants(bins_total):
    order = bin_order(bins_total)
    length = 2 * bins_total
    weights = np.where(order == 0, 1.0, 2.0)[:, None]
    odd = 2 * np.arange(LAGS // 2) + 1
    phase = np.pi / length * ((order[:, None] * odd[None, :]) % (2 * length))
    cos_table, sin_table = (
        np.stack([part.reshape(-1, CHUNK, LAGS // 2) for part in split_table(weights * wave)], axis=1).reshape(
            2 * bins_total, LAGS // 2
        )
        for wave in (np.cos(phase), np.sin(phase))
    )
    shift = np.pi / length * order
    shift_table = np.zeros((8, bins_total), np.float32)
    shift_table[0] = np.cos(shift)
    shift_table[1] = np.sin(shift)
    return cos_table, sin_table, shift_table


def split_value(value):
    high = value.astype(jnp.bfloat16)
    low = (value - high.astype(jnp.float32)).astype(jnp.bfloat16)
    return high, low


def dot(left, right):
    return jnp.dot(left, right, preferred_element_type=jnp.float32)


def code_kernel(members, segs, unit, place_ref, trace_ref, *out_refs):
    halves = HALVES
    span = trace_ref.shape[2]
    width = out_refs[0].shape[1]
    rows = segs * halves * unit
    for distance in range(2 * len(out_refs)):
        partner = place_ref[0] ^ distance
        half = partner // members
        member = partner % members
        for seg in range(segs):
            pieces = []
            for other in range(halves):
                first = pl.multiple_of(((other ^ half) * members + member) * unit, unit)
                pieces.append(trace_ref[half * segs + seg, pl.ds(first, unit), :])
            coded, power = encode(jnp.concatenate(pieces, axis=0))
            tail = jnp.broadcast_to(power, (coded.shape[0], width - span))
            start = distance % 2 * rows + seg * halves * unit
            out_refs[distance // 2][start : start + halves * unit, :] = to_short(
                jnp.concatenate([coded, tail], axis=1)
            )


def code_traces(place, traces, chan_count):
    local_segs, channels, span = traces.shape
    members = chan_count // HALVES
    segs = local_segs // HALVES
    unit = channels // chan_count
    width = round_up(span + 1, 128)
    rows = 2 * segs * HALVES * unit
    return pl.pallas_call(
        functools.partial(code_kernel, members, segs, unit),
        out_shape=[jax.ShapeDtypeStruct((rows, width), jnp.int16)] * (chan_count // 2),
        in_specs=[pl.BlockSpec(memory_space=pltpu.SMEM), pl.BlockSpec(memory_space=pltpu.VMEM)],
        out_specs=[pl.BlockSpec(memory_space=pltpu.VMEM)] * (chan_count // 2),
        compiler_params=pltpu.CompilerParams(vmem_limit_bytes=SMALL_LIMIT),
        name="code_traces",
    )(place, traces)


def exchange_order(chan_count):
    across = chan_count // 2 // HALVES
    return list(range(across, chan_count // 2)) + list(range(1, across)) + [0]


def fourier_8(x):
    root = math.sqrt(0.5)
    s04, d04 = x[0] + x[4], x[0] - x[4]
    s26, d26 = x[2] + x[6], x[2] - x[6]
    s15, d15 = x[1] + x[5], x[1] - x[5]
    s37, d37 = x[3] + x[7], x[3] - x[7]
    even, odd = s04 + s26, s15 + s37
    plus, minus = root * (d15 + d37), root * (d15 - d37)
    reals = [even + odd, d04 + minus, s04 - s26, d04 - minus, even - odd]
    imags = [None, -(d26 + plus), s37 - s15, d26 - plus, None]
    reals += [reals[8 - k] for k in range(5, 8)]
    imags += [-imags[8 - k] for k in range(5, 8)]
    return reals, imags


def fourier_16(x):
    even_reals, even_imags = fourier_8(x[0::2])
    odd_reals, odd_imags = fourier_8(x[1::2])
    reals = []
    imags = []
    for k in range(9):
        if k % 8 == 0:
            reals.append(even_reals[0] + odd_reals[0] if k == 0 else even_reals[0] - odd_reals[0])
            imags.append(None)
        elif k == 4:
            reals.append(even_reals[4])
            imags.append(-odd_reals[4])
        else:
            cos = math.cos(2.0 * math.pi * k / 16)
            sin = math.sin(2.0 * math.pi * k / 16)
            reals.append(even_reals[k] + (odd_reals[k] * cos + odd_imags[k] * sin))
            imags.append(even_imags[k] + (odd_imags[k] * cos - odd_reals[k] * sin))
    reals += [reals[16 - k] for k in range(9, 16)]
    imags += [-imags[16 - k] for k in range(9, 16)]
    return reals, imags


def whiten_kernel(
    span_each,
    places,
    place_ref,
    gate_ref,
    twist_ref,
    tables_far,
    *refs,
):
    block_refs, refs = refs[:-8], refs[-8:]
    out_ref, x_ref, rows_high, rows_low, high_ref, low_ref, mean_ref, arrivals = refs
    copies = []
    for near, (columns, _) in zip((high_ref, low_ref, mean_ref), places):
        copies += table_copies(tables_far, near, columns, arrivals, len(copies))
    for copy in copies:
        copy.start()
    blocks, rows, _ = x_ref.shape
    for number, block_ref in enumerate(block_refs):
        passed, distance = divmod(number, blocks // 2)
        distance = exchange_order(blocks)[distance]
        coded = from_short(block_ref[passed * rows : (passed + 1) * rows, :])
        x_ref[place_ref[0] ^ (2 * distance + passed)] = decode(
            coded[:, :span_each], coded[:, span_each : span_each + 1]
        )
    legs = RADIX // blocks
    span = span_each // legs
    span_pad = rows_high.shape[1]
    fine_pad = high_ref.shape[1] // 2
    fine = span // 2
    whole = fine // 128 * 128
    bins_total = fine * RADIX
    if span_pad > span:
        start = span // 128 * 128
        empty = jnp.zeros((rows_high.shape[0], span_pad - start), jnp.bfloat16)
        rows_high[:, start:] = empty
        rows_low[:, start:] = empty
    x = [x_ref[i // legs][:, i % legs * span : (i % legs + 1) * span] for i in range(RADIX)]
    reals, imags = fourier_16(x)
    for k in range(RADIX):
        real = reals[k]
        imag = imags[k]
        cos = twist_ref[k : k + 1, :]
        sin = twist_ref[RADIX + k : RADIX + k + 1, :]
        if imag is None:
            twisted = (real * cos, -(real * sin))
        else:
            twisted = (real * cos + imag * sin, imag * cos - real * sin)
        for part, value in enumerate(twisted):
            high, low = split_value(value)
            start = (part * RADIX + k) * rows
            rows_high[start : start + rows, :span] = high
            rows_low[start : start + rows, :span] = low
    for copy in copies:
        copy.wait()
    half = RADIX * rows
    table_high = high_ref[...]
    left_high = rows_high[...]
    product = dot(left_high, table_high) + dot(left_high, low_ref[...]) + dot(rows_low[...], table_high)
    real = product[:half, :fine_pad] + product[half:, fine_pad:]
    imag = product[half:, :fine_pad] - product[:half, fine_pad:]
    magnitude = jnp.sqrt(real * real + imag * imag)
    total = magnitude[:rows]
    for k in range(1, RADIX):
        total = total + magnitude[k * rows : (k + 1) * rows]
    first = total.astype(jnp.bfloat16)
    second, third = split_value(total - first.astype(jnp.float32))
    mean = mean_ref[...]
    level = dot(first, mean) + (dot(second, mean) + dot(third, mean)) + EPSILON
    inverse = 1.0 / level
    gate = gate_ref[...]
    for part, value in ((0, real), (1, imag)):
        white = [
            (value[k * rows : (k + 1) * rows] * inverse).astype(jnp.bfloat16).astype(jnp.float32) * gate
            for k in range(RADIX)
        ]
        pieces = [piece[:, :whole] for piece in white]
        if fine > whole:
            pieces.append(jnp.concatenate([piece[:, whole:fine] for piece in white], axis=1))
        start = part * bins_total
        out_ref[:, start : start + bins_total] = jnp.concatenate(pieces, axis=1).astype(jnp.bfloat16)


def whiten(place, blocks, gate, tables, span_each):
    rows = blocks[0].shape[0] // 2
    length = len(blocks) * span_each
    high, low, mean = fourier_constants(length)
    places = all_tables(length)[1][:3]
    span_pad = high.shape[0]
    wide = 2 * RADIX * rows
    return pl.pallas_call(
        functools.partial(whiten_kernel, span_each, places),
        out_shape=jax.ShapeDtypeStruct((rows, length), jnp.bfloat16),
        scratch_shapes=[
            pltpu.VMEM((len(blocks), rows, span_each), jnp.float32),
            pltpu.VMEM((wide, span_pad), jnp.bfloat16),
            pltpu.VMEM((wide, span_pad), jnp.bfloat16),
        ]
        + [pltpu.VMEM(c.shape, jnp.bfloat16) for c in (high, low, mean)]
        + [pltpu.SemaphoreType.DMA((sum(len(columns) for columns, _ in places),))],
        in_specs=[pl.BlockSpec(memory_space=pltpu.SMEM)]
        + [pl.BlockSpec(memory_space=pltpu.VMEM)] * 2
        + [pl.BlockSpec(memory_space=pl.ANY)]
        + [pl.BlockSpec(memory_space=pltpu.VMEM)] * len(blocks),
        compiler_params=pltpu.CompilerParams(vmem_limit_bytes=VMEM_LIMIT),
        cost_estimate=pl.CostEstimate(
            flops=6 * wide * span_pad * span_pad, bytes_accessed=6 * 1024 * 1024, transcendentals=0
        ),
        name="whiten",
    )(place, gate, twists_of(length), tables, *blocks)


def encode(value):
    peak = jnp.maximum(jnp.max(jnp.abs(value), axis=1, keepdims=True), 1e-30)
    power = jnp.ceil(jnp.log2(peak) * FINENESS)
    return jnp.round(value * (STEPS * jnp.exp2(power * (-1.0 / FINENESS)))), power


def decode(coded, power):
    return coded * (jnp.exp2(power * (1.0 / FINENESS)) * (1.0 / STEPS))


def to_short(value):
    return value.astype(jnp.int32).astype(jnp.int16)


def from_short(value):
    return value.astype(jnp.int32).astype(jnp.float32)


def place_powers(powers, power, index):
    lanes = lax.broadcasted_iota(jnp.int32, powers.shape, 1)
    return jnp.where(lanes == index, power, powers)


def correlate_kernel(segs, own, first_own, unit, earlier, table_rows, *refs):
    final = earlier is not None
    if final:
        map_ref, previous, refs = refs[0], refs[1 : 1 + earlier], refs[1 + earlier :]
    own_ref, even_ref, odd_ref, shift_ref, tables_far = refs[:5]
    left_first, left_second, total_even, total_odd, tables, arrivals = refs[-6:]
    outs = refs[5:-6]
    rows, length = own_ref.shape
    bins_total = length // 2
    chunks = bins_total // CHUNK
    seg_rows = rows // segs
    half_lags = LAGS // 2
    unit_tiles = seg_rows // 8
    tiles = 2 * unit_tiles
    each = tiles * 8

    def table_copy(number, part):
        size = tables.shape[2]
        start = table_rows[part] + number * size
        if not isinstance(number, int):
            start = pl.multiple_of(start, BLOCK)
        return pltpu.make_async_copy(
            tables_far.at[pl.ds(start, size)], tables.at[number, part], arrivals.at[number, part]
        )

    def parts_of(ref, number):
        base = number * CHUNK
        if not isinstance(number, int):
            base = pl.multiple_of(base, BLOCK)
        real = ref[:, pl.ds(base, CHUNK)].astype(jnp.float32)
        imag = ref[:, pl.ds(base + bins_total, CHUNK)].astype(jnp.float32)
        return base, real, imag

    def products(number, left_parts):
        base, raw_real, raw_imag = parts_of(own_ref, number)
        shift_cos = shift_ref[0:1, pl.ds(base, CHUNK)]
        shift_sin = shift_ref[1:2, pl.ds(base, CHUNK)]
        own_real = raw_real * shift_cos + raw_imag * shift_sin
        own_imag = raw_imag * shift_cos - raw_real * shift_sin
        mine = (own_real, own_imag - own_real, own_real + own_imag)
        theirs = []
        for ref in (even_ref, odd_ref):
            _, a, b = parts_of(ref, number)
            theirs.append((a - b, a, b))
        for lane in range(0, CHUNK, 128):
            lanes = slice(lane, lane + 128)
            source = [
                [
                    [
                        theirs[tile // unit_tiles][part][
                            seg * seg_rows + tile % unit_tiles * 8 : seg * seg_rows + tile % unit_tiles * 8 + 8, lanes
                        ]
                        for part in range(3)
                    ]
                    for seg in range(segs)
                ]
                for tile in range(tiles)
            ]
            for channel in range(own):
                row = [
                    [
                        mine[part][
                            seg * seg_rows + first_own + channel : seg * seg_rows + first_own + channel + 1, lanes
                        ]
                        for part in range(3)
                    ]
                    for seg in range(segs)
                ]
                results = ([], [])
                for tile in range(tiles):
                    sums = [None, None, None]
                    for seg in range(segs):
                        for part in range(3):
                            term = row[seg][part] * source[tile][seg][part]
                            sums[part] = term if sums[part] is None else sums[part] + term
                    results[0].append(sums[0] + sums[2])
                    results[1].append(sums[0] + sums[1])
                for part in range(2):
                    left_parts[part, channel * each : (channel + 1) * each, lanes] = jnp.concatenate(
                        results[part], axis=0
                    ).astype(jnp.bfloat16)

    def add_lags(number, left_parts):
        for part, total in ((0, total_even), (1, total_odd)):
            left = left_parts[part]
            total[...] += dot(jnp.concatenate([left, left], axis=1), tables[number, part])

    def arrive(number):
        for part in range(2):
            table_copy(number, part).wait()

    for number in range(2):
        for part in range(2):
            table_copy(number, part).start()
    total_even[...] = jnp.zeros_like(total_even)
    total_odd[...] = jnp.zeros_like(total_odd)
    products(0, left_first)

    def body(index, carry):
        for ahead in range(2):
            for part in range(2):
                table_copy(2 * index + 2 + ahead, part).start()
        arrive(2 * index)
        add_lags(2 * index, left_first)
        products(2 * index + 1, left_second)
        arrive(2 * index + 1)
        add_lags(2 * index + 1, left_second)
        products(2 * index + 2, left_first)
        return carry

    lax.fori_loop(0, chunks // 2 - 1, body, 0)
    arrive(chunks - 2)
    add_lags(chunks - 2, left_first)
    products(chunks - 1, left_second)
    arrive(chunks - 1)
    add_lags(chunks - 1, left_second)

    both = jnp.concatenate([total_even[...], total_odd[...]], axis=1)
    if not final:
        for index, out_ref in enumerate(outs):
            out_ref[...] = both[index * unit * each : (index + 1) * unit * each]
        return
    here_ref, sent_refs = outs[0], outs[1:]
    each_out = here_ref.shape[0]
    picked_rows = map_ref.shape[0]
    depth = unit * each
    columns = lax.broadcasted_iota(jnp.int32, (picked_rows, depth), 1)
    wanted = map_ref[...]
    picked = None
    for number, value in enumerate([ref[...] for ref in previous] + [both]):
        choice = (columns + number * depth == wanted).astype(jnp.float32).astype(jnp.bfloat16)
        for piece in split_value(value):
            product = dot(choice, piece)
            picked = product if picked is None else picked + product
    here_ref[...] = picked[:each_out]
    coded, power = encode(picked[each_out:])
    pair = 2 * own
    for place, sent_ref in enumerate(sent_refs):
        base = place * each_out
        sent_ref[:each_out, :] = to_short(coded[base : base + each_out])
        powers = jnp.zeros((pair, LAGS), jnp.float32)
        for index in range(each_out // pair):
            start = base + index * pair
            powers = place_powers(powers, power[start : start + pair], index)
        sent_ref[each_out:, :] = to_short(powers)


def correlate(own_white, even_white, odd_white, tables, segs, unit, previous=None, half=0, source_map=None, places=0):
    rows, length = own_white.shape
    bins_total = length // 2
    final = previous is not None
    seg_rows = rows // segs
    own = unit if final else seg_rows
    first_own = half * unit if final else 0
    each = 2 * seg_rows
    out_rows = own * each
    chunks = bins_total // CHUNK
    shift_table = lag_constants(bins_total)[2]
    table_rows = [columns[0] for columns, _ in all_tables(length)[1][3:]]
    near = pl.BlockSpec(memory_space=pltpu.VMEM)
    in_specs = [near] * 4 + [pl.BlockSpec(memory_space=pl.ANY)]
    operands = [own_white, even_white, odd_white, jnp.asarray(shift_table), tables]
    part_shape = (unit * each, LAGS)
    scratch = [
        pltpu.VMEM((2, out_rows, CHUNK), jnp.bfloat16),
        pltpu.VMEM((2, out_rows, CHUNK), jnp.bfloat16),
        pltpu.VMEM((out_rows, LAGS // 2), jnp.float32),
        pltpu.VMEM((out_rows, LAGS // 2), jnp.float32),
        pltpu.VMEM((chunks, 2, 2 * CHUNK, LAGS // 2), jnp.bfloat16),
        pltpu.SemaphoreType.DMA((chunks, 2)),
    ]
    if not final:
        earlier = None
        out_shape = [jax.ShapeDtypeStruct(part_shape, jnp.float32)] * (own // unit)
    else:
        earlier = len(previous)
        in_specs = [near] * (1 + earlier) + in_specs
        operands = [source_map] + list(previous) + operands
        here_rows = source_map.shape[0] // places
        sent_shape = (here_rows + 2 * own, LAGS)
        out_shape = [jax.ShapeDtypeStruct((here_rows, LAGS), jnp.float32)]
        out_shape += [jax.ShapeDtypeStruct(sent_shape, jnp.int16)] * (places - 1)
    return pl.pallas_call(
        functools.partial(correlate_kernel, segs, own, first_own, unit, earlier, table_rows),
        out_shape=out_shape,
        in_specs=in_specs,
        out_specs=[near] * len(out_shape),
        scratch_shapes=scratch,
        compiler_params=pltpu.CompilerParams(vmem_limit_bytes=VMEM_LIMIT),
        cost_estimate=pl.CostEstimate(
            flops=4 * out_rows * bins_total * LAGS, bytes_accessed=12 * 1024 * 1024, transcendentals=0
        ),
        name="correlate",
    )(*operands)


def total_kernel(unit, here_ref, *refs):
    scale_ref = None
    if refs[-2].shape[1] == 1:
        scale_ref, received, out_ref = refs[-2], refs[:-2], refs[-1]
    else:
        received, out_ref = refs[:-1], refs[-1]
    pair = 2 * unit
    here_rows = here_ref.shape[0]
    steps = [from_short(ref[here_rows : here_rows + pair, :]) for ref in received]
    powers = jnp.zeros((pair, LAGS), jnp.float32)
    values = []
    for index in range(here_rows // pair):
        where = slice(index * pair, (index + 1) * pair)
        value = here_ref[where, :]
        for ref, step in zip(received, steps):
            value = value + decode(from_short(ref[where, :]), step[:, index : index + 1])
        if scale_ref is None:
            coded, power = encode(value)
            out_ref[where, :] = to_short(coded)
            powers = place_powers(powers, power, index)
        else:
            values.append(value * scale_ref[where, :])
    if scale_ref is None:
        out_ref[here_rows:, :] = to_short(powers)
        return
    half_lags = LAGS // 2
    value = jnp.concatenate(values, axis=0)
    even = value[:, :half_lags]
    odd = value[:, half_lags:]
    row_ids = lax.broadcasted_iota(jnp.int32, (half_lags, half_lags), 0)
    column_ids = lax.broadcasted_iota(jnp.int32, (half_lags, half_lags), 1)
    turn = (row_ids + column_ids == half_lags - 1).astype(jnp.float32).astype(jnp.bfloat16)
    back = even + odd
    first = back.astype(jnp.bfloat16)
    second, third = split_value(back - first.astype(jnp.float32))
    out_ref[:, :half_lags] = dot(first, turn) + (dot(second, turn) + dot(third, turn))
    out_ref[:, half_lags:] = even - odd


def total(here, received, unit, scale=None):
    if scale is None:
        out_shape = jax.ShapeDtypeStruct(received[0].shape, jnp.int16)
    else:
        out_shape = jax.ShapeDtypeStruct(here.shape, jnp.float32)
    return pl.pallas_call(
        functools.partial(total_kernel, unit),
        out_shape=out_shape,
        compiler_params=pltpu.CompilerParams(vmem_limit_bytes=SMALL_LIMIT),
        name="total",
    )(here, *received, *([] if scale is None else [scale]))


def swap(value, axis, size, distance):
    return lax.ppermute(value, axis, [(i, i ^ distance) for i in range(size)])


def local(traces, sources, validity):
    chan_count = lax.axis_size("chan")
    seg_count = lax.axis_size("seg")
    chan_index = lax.axis_index("chan")
    seg_index = lax.axis_index("seg")
    local_segs, channels, span = traces.shape
    length = span * chan_count
    unit = channels // chan_count
    halves = HALVES
    members = chan_count // halves
    segs = local_segs // halves
    own = unit * halves
    rows = segs * own
    source_total = sources.shape[0]
    rows_each = source_total // seg_count
    half_index = chan_index // members
    member_index = chan_index % members
    valid = validity.astype(jnp.float32)

    place = chan_index.astype(jnp.int32).reshape(1)
    tables = jnp.asarray(all_tables(length)[0])
    coded = code_traces(place, traces, chan_count)
    order = exchange_order(chan_count)
    blocks = [swap(coded[d], "chan", chan_count, 2 * d) if d else coded[0] for d in order]
    blocks += [swap(block, "chan", chan_count, 1) for block in blocks]
    tables = jnp.asarray(all_tables(length)[0])

    valid_local = lax.dynamic_slice_in_dim(valid, seg_index * local_segs + half_index * segs, segs, 0)
    valid_own = lax.dynamic_index_in_dim(
        valid_local.reshape(segs, halves, members, unit), member_index, 2, keepdims=False
    )
    valid_own = jnp.take(valid_own, jnp.arange(halves) ^ half_index, axis=1)

    units = sources // unit
    where = (units % members) ^ member_index
    where = (where * halves + ((units // members) ^ half_index)) * unit + sources % unit
    places = jnp.arange(seg_count) ^ seg_index
    where = jnp.take(where.reshape(seg_count, rows_each), places, axis=0).reshape(-1, 1)
    each = 2 * own
    channel = jnp.arange(unit, dtype=jnp.int32)[None, :]
    source_map = (where // each * (unit * each) + channel * each + where % each).reshape(-1, 1)

    gate, source_map = lax.optimization_barrier((valid_own.reshape(rows, 1), source_map))
    own_white = whiten(place, blocks, gate, tables, span)

    evens = [own_white] + [swap(own_white, "chan", chan_count, d) for d in range(2, members, 2)]
    previous = []
    for number, even_white in enumerate(evens[:-1]):
        odd_white = swap(even_white, "chan", chan_count, 1)
        previous.append(correlate(own_white, even_white, odd_white, tables, segs, unit))
        evens[number + 1], previous[-1] = lax.optimization_barrier((evens[number + 1], previous[-1]))
    odd_white = swap(evens[-1], "chan", chan_count, 1)

    source_onehot = (sources[:, None] == jnp.arange(channels, dtype=jnp.int32)[None, :]).astype(jnp.float32)
    source_rows = lax.dynamic_slice_in_dim(source_onehot, seg_index * rows_each, rows_each, 0)
    valid_columns = lax.dynamic_slice_in_dim(valid, chan_index * unit, unit, 1)
    source_columns = jnp.dot(valid, source_rows.T, preferred_element_type=jnp.float32)
    pairs = jnp.dot(source_columns.T, valid_columns, preferred_element_type=jnp.float32)
    scale = lax.rsqrt(float(length) * jnp.maximum(pairs, 1.0)).reshape(rows_each * unit, 1)

    arrived = []
    for half in range(halves - 1, -1, -1):
        parts = [part[half] for part in previous]
        here, *sent = correlate(
            own_white, evens[-1], odd_white, tables, segs, unit, parts, half, source_map, seg_count
        )
        if arrived:
            arrived[-1], *sent = lax.optimization_barrier((arrived[-1], *sent))
        received = [swap(piece, "seg", seg_count, index + 1) for index, piece in enumerate(sent)]
        if half > 0:
            arrived.append(total(here, received, unit))
    arrived = [
        swap(piece, "chan", chan_count, (halves - 1 - index) * members) for index, piece in enumerate(arrived)
    ]
    result = total(here, arrived + received, unit, scale)
    return result.reshape(rows_each, unit, LAGS)


def solution(mesh):
    in_specs = (P("seg", None, "chan"), P(), P())
    out_specs = P("seg", "chan", None)
    return jax.shard_map(local, mesh=mesh, in_specs=in_specs, out_specs=out_specs, check_vma=False)
```

profile of v0, /device:TPU:0, one launch (start us, length us, event | category | flops | bytes accessed | tf_op | source)
XLA Modules:
  0.0 67.2 jit_solution(4762025322741363474)
XLA Ops:
  0.0 1.2 %copy-done = f32[4,64,960]{2,1,0:T(8,128)S(1)} copy-done((f32[4,64,960]{2,1,0:T(8,128)S(1)}, f32[4,64,960]{2,1,0:T(8,128)}, u32[]{:S(2)}) %copy-start) | copy-done | bytes 983064
  1.5 4.1 %collective-permute-start = (s16[64,1024]{1,0:T(8,128)(2,1)S(1)}, s16[64,1024]{1,0:T(8,128)(2,1)S(1)}, u32[]{:S(2)}, u32[]{:S(2)}) collective-permute-start(s16[64,1024]{1,0:T(8,128)(2,1)S(1)} %get-tuple-element.30), channel_id=1, source_target_pairs={{0,16},{4,20},{8,24},{12,28},{16,0},{20,4},{24,8},{28,12},{1,17},{... | collective-permute-start | bytes 393224 | tf_op jit(solution)/shard_map/ppermute | solution.py:591
  5.6 1.3 %collective-permute-start.1 = (s16[64,1024]{1,0:T(8,128)(2,1)S(1)}, s16[64,1024]{1,0:T(8,128)(2,1)S(1)}, u32[]{:S(2)}, u32[]{:S(2)}) collective-permute-start(s16[64,1024]{1,0:T(8,128)(2,1)S(1)} %get-tuple-element.31), channel_id=1, source_target_pairs={{0,24},{4,28},{8,16},{12,20},{16,8},{20,12},{24,0},{28,4},{1,25},{... | collective-permute-start | bytes 393224 | tf_op jit(solution)/shard_map/ppermute | solution.py:591
  7.2 0.7 %fusion.18 = s32[64]{0:T(128)S(1)} fusion(s32[64]{0:T(128)} %param.8, s32[]{:T(128)S(6)} %select_n.137, s32[]{:T(128)S(6)} %select_n.140), kind=kLoop, calls=%fused_computation.43 | loop fusion | flops 2816 | bytes 520 | tf_op jit(solution)/shard_map/add | solution.py:629
  8.8 0.7 %convert_element_type.9 = f32[16,64]{1,0:T(8,128)S(1)} convert(s32[16,64]{1,0:T(8,128)} %param.9) | non-fusion elementwise | flops 1024 | bytes 8192 | tf_op jit(solution)/shard_map/convert_element_type | solution.py:611
  9.6 0.6 gather_fusion
  10.3 5.3 %collective-permute-done.refs_0_ = s16[64,1024]{1,0:T(8,128)(2,1)S(1)} collective-permute-done((s16[64,1024]{1,0:T(8,128)(2,1)S(1)}, s16[64,1024]{1,0:T(8,128)(2,1)S(1)}, u32[]{:S(2)}, u32[]{:S(2)}) %collective-permute-start) | collective-permute-done | bytes 131104 | tf_op jit(solution)/shard_map/ppermute | solution.py:591
  17.4 3.7 %whiten.1.refs_0_.refs_1_.refs_2_ = bf16[32,7680]{1,0:T(8,128)(2,1)S(1)} custom-call(s32[1]{0:T(128)} %bitcast.4.place_ref, f32[32,1]{1,0:T(8,128)S(1)} %copy.13.gate_ref, f32[32,480]{1,0:T(8,128)S(1)} %pad_maximum_fusion.twist_ref, bf16[24576,256]{1,0:T(8,128)(2,1)} %constant.147.clone.tables_far.refs_4_.refs_6_, ...), custom_call_target="tpu_custom_call" | custom-call | flops 1610612736 | bytes 6291456 | tf_op jit(solution)/shard_map/whiten/pallas_call | solution.py:297
  21.4 2.5 %collective-permute-start.7 = (bf16[32,7680]{1,0:T(8,128)(2,1)S(1)}, bf16[32,7680]{1,0:T(8,128)(2,1)S(1)}, u32[]{:S(2)}, u32[]{:S(2)}) collective-permute-start(bf16[32,7680]{1,0:T(8,128)(2,1)S(1)} %whiten.1.refs_0_.refs_1_.refs_2_), channel_id=1, source_target_pairs={{0,8},{4,12},{8,0},{12,4},{16,24},{20,28},{24,16},{28,20},{1,9},{5... | collective-permute-start | bytes 1474568 | tf_op jit(solution)/shard_map/ppermute | solution.py:591
  23.9 6.7 %correlate.3 = (f32[256,512]{1,0:T(8,128)S(1)}, f32[256,512]{1,0:T(8,128)S(1)}) custom-call(bf16[32,7680]{1,0:T(8,128)(2,1)S(1)} %whiten.1.refs_0_.refs_1_.refs_2_, bf16[32,7680]{1,0:T(8,128)(2,1)S(1)} %whiten.1.refs_0_.refs_1_.refs_2_, bf16[32,7680]{1,0:T(8,128)(2,1)S(1)} %collective-permute-done.8.refs_2_, f32[8,3840]{1,0:T(8,128)S(1)} %copy-done.1, ...), custom_call_target="tpu_custom_call" | custom-call | flops 4026531840 | bytes 12582912 | tf_op jit(solution)/shard_map/correlate/pallas_call | solution.py:524
  30.6 4.9 %collective-permute-done.7.refs_3_ = bf16[32,7680]{1,0:T(8,128)(2,1)S(1)} collective-permute-done((bf16[32,7680]{1,0:T(8,128)(2,1)S(1)}, bf16[32,7680]{1,0:T(8,128)(2,1)S(1)}, u32[]{:S(2)}, u32[]{:S(2)}) %collective-permute-start.7) | collective-permute-done | bytes 491552 | tf_op jit(solution)/shard_map/ppermute | solution.py:591
  35.7 1.6 %collective-permute-done.9.refs_4_ = bf16[32,7680]{1,0:T(8,128)(2,1)S(1)} collective-permute-done((bf16[32,7680]{1,0:T(8,128)(2,1)S(1)}, bf16[32,7680]{1,0:T(8,128)(2,1)S(1)}, u32[]{:S(2)}, u32[]{:S(2)}) %collective-permute-start.9) | collective-permute-done | bytes 491552 | tf_op jit(solution)/shard_map/ppermute | solution.py:591
  37.3 5.4 %correlate.5 = (f32[128,512]{1,0:T(8,128)S(1)}, s16[144,512]{1,0:T(8,128)(2,1)S(1)}, s16[144,512]{1,0:T(8,128)(2,1)S(1)}, s16[144,512]{1,0:T(8,128)(2,1)S(1)}) custom-call(s32[512,1]{1,0:T(8,128)S(1)} %copy.14.refs_0_, f32[256,512]{1,0:T(8,128)S(1)} %get-tuple-element.39.refs_1_, bf16[32,7680]{1,0:T(8,128)(2,1)S(1)} %whiten.1.refs_0_.refs_1_.refs_2_, ...), custom_call_target="tpu_custom_call" | custom-call | flops 2013265920 | bytes 12582912 | tf_op jit(solution)/shard_map/correlate/pallas_call | solution.py:524
  42.7 1.6 %collective-permute-start.10 = (s16[144,512]{1,0:T(8,128)(2,1)S(1)}, s16[144,512]{1,0:T(8,128)(2,1)S(1)}, u32[]{:S(2)}, u32[]{:S(2)}) collective-permute-start(s16[144,512]{1,0:T(8,128)(2,1)S(1)} %get-tuple-element.41), channel_id=1, source_target_pairs={{0,1},{1,0},{2,3},{3,2},{4,5},{5,4},{6,7},{7,6},{8,9},{9,8},{10,11... | collective-permute-start | bytes 442376 | tf_op jit(solution)/shard_map/ppermute | solution.py:591
  44.3 1.5 %collective-permute-start.11 = (s16[144,512]{1,0:T(8,128)(2,1)S(1)}, s16[144,512]{1,0:T(8,128)(2,1)S(1)}, u32[]{:S(2)}, u32[]{:S(2)}) collective-permute-start(s16[144,512]{1,0:T(8,128)(2,1)S(1)} %get-tuple-element.42), channel_id=1, source_target_pairs={{0,2},{1,3},{2,0},{3,1},{4,6},{5,7},{6,4},{7,5},{8,10},{9,11},{10,... | collective-permute-start | bytes 442376 | tf_op jit(solution)/shard_map/ppermute | solution.py:591
  46.3 5.4 %correlate.4 = (f32[128,512]{1,0:T(8,128)S(1)}, s16[144,512]{1,0:T(8,128)(2,1)S(1)}, s16[144,512]{1,0:T(8,128)(2,1)S(1)}, s16[144,512]{1,0:T(8,128)(2,1)S(1)}) custom-call(s32[512,1]{1,0:T(8,128)S(1)} %copy.14.refs_0_, f32[256,512]{1,0:T(8,128)S(1)} %get-tuple-element.36.refs_1_, bf16[32,7680]{1,0:T(8,128)(2,1)S(1)} %whiten.1.refs_0_.refs_1_.refs_2_, ...), custom_call_target="tpu_custom_call" | custom-call | flops 2013265920 | bytes 12582912 | tf_op jit(solution)/shard_map/correlate/pallas_call | solution.py:524
  51.7 1.3 %collective-permute-done.11.refs_1_ = s16[144,512]{1,0:T(8,128)(2,1)S(1)} collective-permute-done((s16[144,512]{1,0:T(8,128)(2,1)S(1)}, s16[144,512]{1,0:T(8,128)(2,1)S(1)}, u32[]{:S(2)}, u32[]{:S(2)}) %collective-permute-start.11) | collective-permute-done | bytes 147488 | tf_op jit(solution)/shard_map/ppermute | solution.py:591
  53.5 3.7 %collective-permute-start.13 = (s16[144,512]{1,0:T(8,128)(2,1)S(1)}, s16[144,512]{1,0:T(8,128)(2,1)S(1)}, u32[]{:S(2)}, u32[]{:S(2)}) collective-permute-start(s16[144,512]{1,0:T(8,128)(2,1)S(1)} %total.2), channel_id=1, source_target_pairs={{0,16},{4,20},{8,24},{12,28},{16,0},{20,4},{24,8},{28,12},{1,17},{... | collective-permute-start | bytes 442376 | tf_op jit(solution)/shard_map/ppermute | solution.py:591
  57.3 1.2 %collective-permute-start.14 = (s16[144,512]{1,0:T(8,128)(2,1)S(1)}, s16[144,512]{1,0:T(8,128)(2,1)S(1)}, u32[]{:S(2)}, u32[]{:S(2)}) collective-permute-start(s16[144,512]{1,0:T(8,128)(2,1)S(1)} %get-tuple-element.48), channel_id=1, source_target_pairs={{0,1},{1,0},{2,3},{3,2},{4,5},{5,4},{6,7},{7,6},{8,9},{9,8},{10,11... | collective-permute-start | bytes 442376 | tf_op jit(solution)/shard_map/ppermute | solution.py:591
  58.5 0.8 %collective-permute-start.15 = (s16[144,512]{1,0:T(8,128)(2,1)S(1)}, s16[144,512]{1,0:T(8,128)(2,1)S(1)}, u32[]{:S(2)}, u32[]{:S(2)}) collective-permute-start(s16[144,512]{1,0:T(8,128)(2,1)S(1)} %get-tuple-element.49), channel_id=1, source_target_pairs={{0,2},{1,3},{2,0},{3,1},{4,6},{5,7},{6,4},{7,5},{8,10},{9,11},{10,... | collective-permute-start | bytes 442376 | tf_op jit(solution)/shard_map/ppermute | solution.py:591
  59.3 1.4 %collective-permute-start.16 = (s16[144,512]{1,0:T(8,128)(2,1)S(1)}, s16[144,512]{1,0:T(8,128)(2,1)S(1)}, u32[]{:S(2)}, u32[]{:S(2)}) collective-permute-start(s16[144,512]{1,0:T(8,128)(2,1)S(1)} %get-tuple-element.50), channel_id=1, source_target_pairs={{0,3},{1,2},{2,1},{3,0},{4,7},{5,6},{6,5},{7,4},{8,11},{9,10},{10,... | collective-permute-start | bytes 442376 | tf_op jit(solution)/shard_map/ppermute | solution.py:591
  61.2 2.4 %collective-permute-done.13.refs_0_ = s16[144,512]{1,0:T(8,128)(2,1)S(1)} collective-permute-done((s16[144,512]{1,0:T(8,128)(2,1)S(1)}, s16[144,512]{1,0:T(8,128)(2,1)S(1)}, u32[]{:S(2)}, u32[]{:S(2)}) %collective-permute-start.13) | collective-permute-done | bytes 147488 | tf_op jit(solution)/shard_map/ppermute | solution.py:591
  63.8 2.4 %collective-permute-done.15.refs_2_ = s16[144,512]{1,0:T(8,128)(2,1)S(1)} collective-permute-done((s16[144,512]{1,0:T(8,128)(2,1)S(1)}, s16[144,512]{1,0:T(8,128)(2,1)S(1)}, u32[]{:S(2)}, u32[]{:S(2)}) %collective-permute-start.15) | collective-permute-done | bytes 147488 | tf_op jit(solution)/shard_map/ppermute | solution.py:591
  66.2 1.1 %total.3 = f32[128,512]{1,0:T(8,128)} custom-call(f32[128,512]{1,0:T(8,128)S(1)} %get-tuple-element.38.here_ref, s16[144,512]{1,0:T(8,128)(2,1)S(1)} %collective-permute-done.13.refs_0_, s16[144,512]{1,0:T(8,128)(2,1)S(1)} %collective-permute-done.14.refs_1_, s16[144,512]{1,0:T(8,128)(2,1)S(1)} %collective-permute-done.15.refs_2_, ...), custom_call_target="tpu_custom_call" | custom-call | tf_op jit(solution)/shard_map/total/pallas_call | solution.py:582
  (55 shorter events, 5.5 us)
Async XLA Ops:
  0.0 1.2 %copy-start = (f32[4,64,960]{2,1,0:T(8,128)S(1)}, f32[4,64,960]{2,1,0:T(8,128)}, u32[]{:S(2)}) copy-start(f32[4,64,960]{2,1,0:T(8,128)} %trace_ref.1) | copy-start | bytes 2949124
  1.2 22.7 %copy-start.1 = (f32[8,3840]{1,0:T(8,128)S(1)}, f32[8,3840]{1,0:T(8,128)}, u32[]{:S(2)}) copy-start(f32[8,3840]{1,0:T(8,128)} %constant.148.clone.refs_3_.refs_5_) | copy-start | bytes 368644
  1.5 14.1 %collective-permute-start = (s16[64,1024]{1,0:T(8,128)(2,1)S(1)}, s16[64,1024]{1,0:T(8,128)(2,1)S(1)}, u32[]{:S(2)}, u32[]{:S(2)}) collective-permute-start(s16[64,1024]{1,0:T(8,128)(2,1)S(1)} %get-tuple-element.30), channel_id=1, source_target_pairs={{0,16},{4,20},{8,24},{12,28},{16,0},{20,4},{24,8},{28,12},{1,17},{... | collective-permute-start | bytes 393224 | tf_op jit(solution)/shard_map/ppermute | solution.py:591
  5.6 10.0 %collective-permute-start.1 = (s16[64,1024]{1,0:T(8,128)(2,1)S(1)}, s16[64,1024]{1,0:T(8,128)(2,1)S(1)}, u32[]{:S(2)}, u32[]{:S(2)}) collective-permute-start(s16[64,1024]{1,0:T(8,128)(2,1)S(1)} %get-tuple-element.31), channel_id=1, source_target_pairs={{0,24},{4,28},{8,16},{12,20},{16,8},{20,12},{24,0},{28,4},{1,25},{... | collective-permute-start | bytes 393224 | tf_op jit(solution)/shard_map/ppermute | solution.py:591
  6.9 9.2 %collective-permute-start.2 = (s16[64,1024]{1,0:T(8,128)(2,1)S(1)}, s16[64,1024]{1,0:T(8,128)(2,1)S(1)}, u32[]{:S(2)}, u32[]{:S(2)}) collective-permute-start(s16[64,1024]{1,0:T(8,128)(2,1)S(1)} %get-tuple-element.32), channel_id=1, source_target_pairs={{0,8},{4,12},{8,0},{12,4},{16,24},{20,28},{24,16},{28,20},{1,9},{5... | collective-permute-start | bytes 393224 | tf_op jit(solution)/shard_map/ppermute | solution.py:591
  7.2 9.4 %collective-permute-start.6 = (s16[64,1024]{1,0:T(8,128)(2,1)S(1)}, s16[64,1024]{1,0:T(8,128)(2,1)S(1)}, u32[]{:S(2)}, u32[]{:S(2)}) collective-permute-start(s16[64,1024]{1,0:T(8,128)(2,1)S(1)} %get-tuple-element.33.refs_3_), channel_id=1, source_target_pairs={{0,4},{4,0},{8,12},{12,8},{16,20},{20,16},{24,28},{28,24},{1,5},{5... | collective-permute-start | bytes 393224 | tf_op jit(solution)/shard_map/ppermute | solution.py:591
  15.6 1.3 %collective-permute-start.3 = (s16[64,1024]{1,0:T(8,128)(2,1)S(1)}, s16[64,1024]{1,0:T(8,128)(2,1)S(1)}, u32[]{:S(2)}, u32[]{:S(2)}) collective-permute-start(s16[64,1024]{1,0:T(8,128)(2,1)S(1)} %collective-permute-done.refs_0_), channel_id=1, source_target_pairs={{0,4},{4,0},{8,12},{12,8},{16,20},{20,16},{24,28},{28,24},{1,5},{5... | collective-permute-start | bytes 393224 | tf_op jit(solution)/shard_map/ppermute | solution.py:591
  15.6 1.5 %collective-permute-start.4 = (s16[64,1024]{1,0:T(8,128)(2,1)S(1)}, s16[64,1024]{1,0:T(8,128)(2,1)S(1)}, u32[]{:S(2)}, u32[]{:S(2)}) collective-permute-start(s16[64,1024]{1,0:T(8,128)(2,1)S(1)} %collective-permute-done.1.refs_1_), channel_id=1, source_target_pairs={{0,4},{4,0},{8,12},{12,8},{16,20},{20,16},{24,28},{28,24},{1,5},{5... | collective-permute-start | bytes 393224 | tf_op jit(solution)/shard_map/ppermute | solution.py:591
  16.1 1.3 %collective-permute-start.5 = (s16[64,1024]{1,0:T(8,128)(2,1)S(1)}, s16[64,1024]{1,0:T(8,128)(2,1)S(1)}, u32[]{:S(2)}, u32[]{:S(2)}) collective-permute-start(s16[64,1024]{1,0:T(8,128)(2,1)S(1)} %collective-permute-done.2.refs_2_), channel_id=1, source_target_pairs={{0,4},{4,0},{8,12},{12,8},{16,20},{20,16},{24,28},{28,24},{1,5},{5... | collective-permute-start | bytes 393224 | tf_op jit(solution)/shard_map/ppermute | solution.py:591
  16.6 19.0 %copy-start.2 = (s32[64]{0:T(128)S(1)}, s32[64]{0:T(128)}, u32[]{:S(2)}) copy-start(s32[64]{0:T(128)} %param.8) | copy-start | bytes 772
  21.1 2.8 %collective-permute-start.8 = (bf16[32,7680]{1,0:T(8,128)(2,1)S(1)}, bf16[32,7680]{1,0:T(8,128)(2,1)S(1)}, u32[]{:S(2)}, u32[]{:S(2)}) collective-permute-start(bf16[32,7680]{1,0:T(8,128)(2,1)S(1)} %whiten.1.refs_0_.refs_1_.refs_2_), channel_id=1, source_target_pairs={{0,4},{4,0},{8,12},{12,8},{16,20},{20,16},{24,28},{28,24},{1,5},{5... | collective-permute-start | bytes 1474568 | tf_op jit(solution)/shard_map/ppermute | solution.py:591
  21.4 14.1 %collective-permute-start.7 = (bf16[32,7680]{1,0:T(8,128)(2,1)S(1)}, bf16[32,7680]{1,0:T(8,128)(2,1)S(1)}, u32[]{:S(2)}, u32[]{:S(2)}) collective-permute-start(bf16[32,7680]{1,0:T(8,128)(2,1)S(1)} %whiten.1.refs_0_.refs_1_.refs_2_), channel_id=1, source_target_pairs={{0,8},{4,12},{8,0},{12,4},{16,24},{20,28},{24,16},{28,20},{1,9},{5... | collective-permute-start | bytes 1474568 | tf_op jit(solution)/shard_map/ppermute | solution.py:591
  35.4 1.9 %collective-permute-start.9 = (bf16[32,7680]{1,0:T(8,128)(2,1)S(1)}, bf16[32,7680]{1,0:T(8,128)(2,1)S(1)}, u32[]{:S(2)}, u32[]{:S(2)}) collective-permute-start(bf16[32,7680]{1,0:T(8,128)(2,1)S(1)} %collective-permute-done.7.refs_3_), channel_id=1, source_target_pairs={{0,4},{4,0},{8,12},{12,8},{16,20},{20,16},{24,28},{28,24},{1,5},{5... | collective-permute-start | bytes 1474568 | tf_op jit(solution)/shard_map/ppermute | solution.py:591
  42.7 9.0 %collective-permute-start.10 = (s16[144,512]{1,0:T(8,128)(2,1)S(1)}, s16[144,512]{1,0:T(8,128)(2,1)S(1)}, u32[]{:S(2)}, u32[]{:S(2)}) collective-permute-start(s16[144,512]{1,0:T(8,128)(2,1)S(1)} %get-tuple-element.41), channel_id=1, source_target_pairs={{0,1},{1,0},{2,3},{3,2},{4,5},{5,4},{6,7},{7,6},{8,9},{9,8},{10,11... | collective-permute-start | bytes 442376 | tf_op jit(solution)/shard_map/ppermute | solution.py:591
  44.3 8.8 %collective-permute-start.11 = (s16[144,512]{1,0:T(8,128)(2,1)S(1)}, s16[144,512]{1,0:T(8,128)(2,1)S(1)}, u32[]{:S(2)}, u32[]{:S(2)}) collective-permute-start(s16[144,512]{1,0:T(8,128)(2,1)S(1)} %get-tuple-element.42), channel_id=1, source_target_pairs={{0,2},{1,3},{2,0},{3,1},{4,6},{5,7},{6,4},{7,5},{8,10},{9,11},{10,... | collective-permute-start | bytes 442376 | tf_op jit(solution)/shard_map/ppermute | solution.py:591
  45.8 7.3 %collective-permute-start.12 = (s16[144,512]{1,0:T(8,128)(2,1)S(1)}, s16[144,512]{1,0:T(8,128)(2,1)S(1)}, u32[]{:S(2)}, u32[]{:S(2)}) collective-permute-start(s16[144,512]{1,0:T(8,128)(2,1)S(1)} %get-tuple-element.43), channel_id=1, source_target_pairs={{0,3},{1,2},{2,1},{3,0},{4,7},{5,6},{6,5},{7,4},{8,11},{9,10},{10,... | collective-permute-start | bytes 442376 | tf_op jit(solution)/shard_map/ppermute | solution.py:591
  53.5 10.1 %collective-permute-start.13 = (s16[144,512]{1,0:T(8,128)(2,1)S(1)}, s16[144,512]{1,0:T(8,128)(2,1)S(1)}, u32[]{:S(2)}, u32[]{:S(2)}) collective-permute-start(s16[144,512]{1,0:T(8,128)(2,1)S(1)} %total.2), channel_id=1, source_target_pairs={{0,16},{4,20},{8,24},{12,28},{16,0},{20,4},{24,8},{28,12},{1,17},{... | collective-permute-start | bytes 442376 | tf_op jit(solution)/shard_map/ppermute | solution.py:591
  57.3 6.5 %collective-permute-start.14 = (s16[144,512]{1,0:T(8,128)(2,1)S(1)}, s16[144,512]{1,0:T(8,128)(2,1)S(1)}, u32[]{:S(2)}, u32[]{:S(2)}) collective-permute-start(s16[144,512]{1,0:T(8,128)(2,1)S(1)} %get-tuple-element.48), channel_id=1, source_target_pairs={{0,1},{1,0},{2,3},{3,2},{4,5},{5,4},{6,7},{7,6},{8,9},{9,8},{10,11... | collective-permute-start | bytes 442376 | tf_op jit(solution)/shard_map/ppermute | solution.py:591
  58.5 7.7 %collective-permute-start.15 = (s16[144,512]{1,0:T(8,128)(2,1)S(1)}, s16[144,512]{1,0:T(8,128)(2,1)S(1)}, u32[]{:S(2)}, u32[]{:S(2)}) collective-permute-start(s16[144,512]{1,0:T(8,128)(2,1)S(1)} %get-tuple-element.49), channel_id=1, source_target_pairs={{0,2},{1,3},{2,0},{3,1},{4,6},{5,7},{6,4},{7,5},{8,10},{9,11},{10,... | collective-permute-start | bytes 442376 | tf_op jit(solution)/shard_map/ppermute | solution.py:591
  59.3 6.8 %collective-permute-start.16 = (s16[144,512]{1,0:T(8,128)(2,1)S(1)}, s16[144,512]{1,0:T(8,128)(2,1)S(1)}, u32[]{:S(2)}, u32[]{:S(2)}) collective-permute-start(s16[144,512]{1,0:T(8,128)(2,1)S(1)} %get-tuple-element.50), channel_id=1, source_target_pairs={{0,3},{1,2},{2,1},{3,0},{4,7},{5,6},{6,5},{7,4},{8,11},{9,10},{10,... | collective-permute-start | bytes 442376 | tf_op jit(solution)/shard_map/ppermute | solution.py:591
where the time goes:
time: 67.6 us; the launch traced here: 67.2 us
  Pallas kernels  22.9 us (34%)
  starting transfers between devices  19.8 us (29%)
  waiting for transfers between devices  18.9 us (28%)
  local copies, waits for them, and re-layouts  3.34 us (5%)
  other arithmetic  1.8 us (3%)
    ppermute x17, starting transfers between devices, swap(): return lax.ppermute(value, axis, [(i, i ^ distance) for i in range(size)])  19.8 us
    ppermute x17, waiting for transfers between devices, swap(): return lax.ppermute(value, axis, [(i, i ^ distance) for i in range(size)])  18.9 us
    pallas_call x3, Pallas kernels, correlate(): pl.pallas_call(functools.partial(correlate_kernel, segs, own, first_own,...  17.5 us
    pallas_call x1, Pallas kernels, whiten(): pl.pallas_call(functools.partial(whiten_kernel, span_each, places), out_s...  3.68 us
    pallas_call x2, Pallas kernels, total(): pl.pallas_call(functools.partial(total_kernel, unit), out_shape=out_shape...  1.56 us
  transfers between devices with their start and end apart: 17, of which 10 were waited for; matrix products, arithmetic and copies ran while one was open for 6% of the time, Pallas kernels for 18%

commit v1 on v0

--- a/solution.py
+++ b/solution.py
@@ -611,7 +611,6 @@
     valid = validity.astype(jnp.float32)
 
     place = chan_index.astype(jnp.int32).reshape(1)
-    tables = jnp.asarray(all_tables(length)[0])
     coded = code_traces(place, traces, chan_count)
     order = exchange_order(chan_count)
     blocks = [swap(coded[d], "chan", chan_count, 2 * d) if d else coded[0] for d in order]
@@ -657,15 +656,10 @@
         here, *sent = correlate(
             own_white, evens[-1], odd_white, tables, segs, unit, parts, half, source_map, seg_count
         )
-        if arrived:
-            arrived[-1], *sent = lax.optimization_barrier((arrived[-1], *sent))
         received = [swap(piece, "seg", seg_count, index + 1) for index, piece in enumerate(sent)]
         if half > 0:
-            arrived.append(total(here, received, unit))
-    arrived = [
-        swap(piece, "chan", chan_count, (halves - 1 - index) * members) for index, piece in enumerate(arrived)
-    ]
-    result = total(here, arrived + received, unit, scale)
+            arrived.append(swap(total(here, received, unit), "chan", chan_count, half * members))
+    result = total(here, received + arrived, unit, scale)
     return result.reshape(rows_each, unit, LAGS)
 
 

time: 67.6 us -> 66.5 us (0.984)
  waiting for transfers between devices: 18.9 us -> 17.7 us
    ppermute x17, waiting for transfers between devices: 18.9 us -> 17.7 us  [swap(): return lax.ppermute(value, axis, [(i, i ^ distance) for i in range(size)])]
  transfers between devices with their start and end apart: 17 -> 17, of which waited for: 10 -> 8; matrix products, arithmetic and copies ran while one was open for 6% -> 6% of each run, Pallas kernels for 18% -> 19%
where the time goes in v1:
time: 66.5 us; the launch traced here: 66.2 us
  Pallas kernels  22.9 us (34%)
  starting transfers between devices  19.9 us (30%)
  waiting for transfers between devices  17.7 us (27%)
  local copies, waits for them, and re-layouts  3.34 us (5%)
  other arithmetic  1.8 us (3%)
    ppermute x17, starting transfers between devices, swap(): return lax.ppermute(value, axis, [(i, i ^ distance) for i in range(size)])  19.9 us
    ppermute x17, waiting for transfers between devices, swap(): return lax.ppermute(value, axis, [(i, i ^ distance) for i in range(size)])  17.7 us
    pallas_call x3, Pallas kernels, correlate(): pl.pallas_call(functools.partial(correlate_kernel, segs, own, first_own,...  17.5 us
    pallas_call x1, Pallas kernels, whiten(): pl.pallas_call(functools.partial(whiten_kernel, span_each, places), out_s...  3.68 us
    pallas_call x2, Pallas kernels, total(): pl.pallas_call(functools.partial(total_kernel, unit), out_shape=out_shape...  1.56 us
  transfers between devices with their start and end apart: 17, of which 8 were waited for; matrix products, arithmetic and copies ran while one was open for 6% of the time, Pallas kernels for 19%

profile of v1, /device:TPU:0, one launch (start us, length us, event | category | flops | bytes accessed | tf_op | source)
XLA Modules:
  0.0 66.2 jit_solution(12834475770435491485)
XLA Ops:
  0.0 1.2 %copy-done = f32[4,64,960]{2,1,0:T(8,128)S(1)} copy-done((f32[4,64,960]{2,1,0:T(8,128)S(1)}, f32[4,64,960]{2,1,0:T(8,128)}, u32[]{:S(2)}) %copy-start) | copy-done | bytes 983064
  1.5 4.1 %collective-permute-start = (s16[64,1024]{1,0:T(8,128)(2,1)S(1)}, s16[64,1024]{1,0:T(8,128)(2,1)S(1)}, u32[]{:S(2)}, u32[]{:S(2)}) collective-permute-start(s16[64,1024]{1,0:T(8,128)(2,1)S(1)} %get-tuple-element.26), channel_id=1, source_target_pairs={{0,16},{4,20},{8,24},{12,28},{16,0},{20,4},{24,8},{28,12},{1,17},{... | collective-permute-start | bytes 393224 | tf_op jit(solution)/shard_map/ppermute | solution.py:591
  5.6 1.3 %collective-permute-start.1 = (s16[64,1024]{1,0:T(8,128)(2,1)S(1)}, s16[64,1024]{1,0:T(8,128)(2,1)S(1)}, u32[]{:S(2)}, u32[]{:S(2)}) collective-permute-start(s16[64,1024]{1,0:T(8,128)(2,1)S(1)} %get-tuple-element.27), channel_id=1, source_target_pairs={{0,24},{4,28},{8,16},{12,20},{16,8},{20,12},{24,0},{28,4},{1,25},{... | collective-permute-start | bytes 393224 | tf_op jit(solution)/shard_map/ppermute | solution.py:591
  7.2 0.7 %fusion.18 = s32[64]{0:T(128)S(1)} fusion(s32[64]{0:T(128)} %param.8, s32[]{:T(128)S(6)} %select_n.137, s32[]{:T(128)S(6)} %select_n.140), kind=kLoop, calls=%fused_computation.43 | loop fusion | flops 2816 | bytes 520 | tf_op jit(solution)/shard_map/add | solution.py:628
  8.0 0.6 gather_fusion.1
  8.8 0.7 %convert_element_type.9 = f32[16,64]{1,0:T(8,128)S(1)} convert(s32[16,64]{1,0:T(8,128)} %param.9) | non-fusion elementwise | flops 1024 | bytes 8192 | tf_op jit(solution)/shard_map/convert_element_type | solution.py:611
  9.6 0.6 gather_fusion
  10.3 5.3 %collective-permute-done.refs_0_ = s16[64,1024]{1,0:T(8,128)(2,1)S(1)} collective-permute-done((s16[64,1024]{1,0:T(8,128)(2,1)S(1)}, s16[64,1024]{1,0:T(8,128)(2,1)S(1)}, u32[]{:S(2)}, u32[]{:S(2)}) %collective-permute-start) | collective-permute-done | bytes 131104 | tf_op jit(solution)/shard_map/ppermute | solution.py:591
  15.6 0.5 collective-permute-start.4
  17.4 3.7 %whiten.1.refs_0_.refs_1_.refs_2_ = bf16[32,7680]{1,0:T(8,128)(2,1)S(1)} custom-call(s32[1]{0:T(128)} %bitcast.4.place_ref, f32[32,1]{1,0:T(8,128)S(1)} %copy.13.gate_ref, f32[32,480]{1,0:T(8,128)S(1)} %pad_maximum_fusion.twist_ref, bf16[24576,256]{1,0:T(8,128)(2,1)} %constant.147.clone.tables_far.refs_4_.refs_6_, ...), custom_call_target="tpu_custom_call" | custom-call | flops 1610612736 | bytes 6291456 | tf_op jit(solution)/shard_map/whiten/pallas_call | solution.py:297
  21.4 2.5 %collective-permute-start.7 = (bf16[32,7680]{1,0:T(8,128)(2,1)S(1)}, bf16[32,7680]{1,0:T(8,128)(2,1)S(1)}, u32[]{:S(2)}, u32[]{:S(2)}) collective-permute-start(bf16[32,7680]{1,0:T(8,128)(2,1)S(1)} %whiten.1.refs_0_.refs_1_.refs_2_), channel_id=1, source_target_pairs={{0,8},{4,12},{8,0},{12,4},{16,24},{20,28},{24,16},{28,20},{1,9},{5... | collective-permute-start | bytes 1474568 | tf_op jit(solution)/shard_map/ppermute | solution.py:591
  23.9 6.7 %correlate.3 = (f32[256,512]{1,0:T(8,128)S(1)}, f32[256,512]{1,0:T(8,128)S(1)}) custom-call(bf16[32,7680]{1,0:T(8,128)(2,1)S(1)} %whiten.1.refs_0_.refs_1_.refs_2_, bf16[32,7680]{1,0:T(8,128)(2,1)S(1)} %whiten.1.refs_0_.refs_1_.refs_2_, bf16[32,7680]{1,0:T(8,128)(2,1)S(1)} %collective-permute-done.8.refs_2_, f32[8,3840]{1,0:T(8,128)S(1)} %copy-done.1, ...), custom_call_target="tpu_custom_call" | custom-call | flops 4026531840 | bytes 12582912 | tf_op jit(solution)/shard_map/correlate/pallas_call | solution.py:524
  30.6 4.9 %collective-permute-done.7.refs_3_ = bf16[32,7680]{1,0:T(8,128)(2,1)S(1)} collective-permute-done((bf16[32,7680]{1,0:T(8,128)(2,1)S(1)}, bf16[32,7680]{1,0:T(8,128)(2,1)S(1)}, u32[]{:S(2)}, u32[]{:S(2)}) %collective-permute-start.7) | collective-permute-done | bytes 491552 | tf_op jit(solution)/shard_map/ppermute | solution.py:591
  35.7 1.6 %collective-permute-done.9.refs_4_ = bf16[32,7680]{1,0:T(8,128)(2,1)S(1)} collective-permute-done((bf16[32,7680]{1,0:T(8,128)(2,1)S(1)}, bf16[32,7680]{1,0:T(8,128)(2,1)S(1)}, u32[]{:S(2)}, u32[]{:S(2)}) %collective-permute-start.9) | collective-permute-done | bytes 491552 | tf_op jit(solution)/shard_map/ppermute | solution.py:591
  37.3 5.4 %correlate.5 = (f32[128,512]{1,0:T(8,128)S(1)}, s16[144,512]{1,0:T(8,128)(2,1)S(1)}, s16[144,512]{1,0:T(8,128)(2,1)S(1)}, s16[144,512]{1,0:T(8,128)(2,1)S(1)}) custom-call(s32[512,1]{1,0:T(8,128)S(1)} %copy.14.refs_0_, f32[256,512]{1,0:T(8,128)S(1)} %get-tuple-element.38.refs_1_, bf16[32,7680]{1,0:T(8,128)(2,1)S(1)} %whiten.1.refs_0_.refs_1_.refs_2_, ...), custom_call_target="tpu_custom_call" | custom-call | flops 2013265920 | bytes 12582912 | tf_op jit(solution)/shard_map/correlate/pallas_call | solution.py:524
  42.7 1.6 %collective-permute-start.13 = (s16[144,512]{1,0:T(8,128)(2,1)S(1)}, s16[144,512]{1,0:T(8,128)(2,1)S(1)}, u32[]{:S(2)}, u32[]{:S(2)}) collective-permute-start(s16[144,512]{1,0:T(8,128)(2,1)S(1)} %get-tuple-element.40), channel_id=1, source_target_pairs={{0,1},{1,0},{2,3},{3,2},{4,5},{5,4},{6,7},{7,6},{8,9},{9,8},{10,11... | collective-permute-start | bytes 442376 | tf_op jit(solution)/shard_map/ppermute | solution.py:591
  44.3 1.5 %collective-permute-start.14 = (s16[144,512]{1,0:T(8,128)(2,1)S(1)}, s16[144,512]{1,0:T(8,128)(2,1)S(1)}, u32[]{:S(2)}, u32[]{:S(2)}) collective-permute-start(s16[144,512]{1,0:T(8,128)(2,1)S(1)} %get-tuple-element.41), channel_id=1, source_target_pairs={{0,2},{1,3},{2,0},{3,1},{4,6},{5,7},{6,4},{7,5},{8,10},{9,11},{10,... | collective-permute-start | bytes 442376 | tf_op jit(solution)/shard_map/ppermute | solution.py:591
  46.3 5.4 %correlate.4 = (f32[128,512]{1,0:T(8,128)S(1)}, s16[144,512]{1,0:T(8,128)(2,1)S(1)}, s16[144,512]{1,0:T(8,128)(2,1)S(1)}, s16[144,512]{1,0:T(8,128)(2,1)S(1)}) custom-call(s32[512,1]{1,0:T(8,128)S(1)} %copy.14.refs_0_, f32[256,512]{1,0:T(8,128)S(1)} %get-tuple-element.32.refs_1_, bf16[32,7680]{1,0:T(8,128)(2,1)S(1)} %whiten.1.refs_0_.refs_1_.refs_2_, ...), custom_call_target="tpu_custom_call" | custom-call | flops 2013265920 | bytes 12582912 | tf_op jit(solution)/shard_map/correlate/pallas_call | solution.py:524
  51.7 1.6 %collective-permute-start.10 = (s16[144,512]{1,0:T(8,128)(2,1)S(1)}, s16[144,512]{1,0:T(8,128)(2,1)S(1)}, u32[]{:S(2)}, u32[]{:S(2)}) collective-permute-start(s16[144,512]{1,0:T(8,128)(2,1)S(1)} %get-tuple-element.35), channel_id=1, source_target_pairs={{0,1},{1,0},{2,3},{3,2},{4,5},{5,4},{6,7},{7,6},{8,9},{9,8},{10,11... | collective-permute-start | bytes 442376 | tf_op jit(solution)/shard_map/ppermute | solution.py:591
  53.2 1.5 %collective-permute-start.11 = (s16[144,512]{1,0:T(8,128)(2,1)S(1)}, s16[144,512]{1,0:T(8,128)(2,1)S(1)}, u32[]{:S(2)}, u32[]{:S(2)}) collective-permute-start(s16[144,512]{1,0:T(8,128)(2,1)S(1)} %get-tuple-element.36), channel_id=1, source_target_pairs={{0,2},{1,3},{2,0},{3,1},{4,6},{5,7},{6,4},{7,5},{8,10},{9,11},{10,... | collective-permute-start | bytes 442376 | tf_op jit(solution)/shard_map/ppermute | solution.py:591
  55.7 3.7 %collective-permute-start.16 = (s16[144,512]{1,0:T(8,128)(2,1)S(1)}, s16[144,512]{1,0:T(8,128)(2,1)S(1)}, u32[]{:S(2)}, u32[]{:S(2)}) collective-permute-start(s16[144,512]{1,0:T(8,128)(2,1)S(1)} %total.2), channel_id=1, source_target_pairs={{0,16},{4,20},{8,24},{12,28},{16,0},{20,4},{24,8},{28,12},{1,17},{... | collective-permute-start | bytes 442376 | tf_op jit(solution)/shard_map/ppermute | solution.py:591
  60.0 1.6 %collective-permute-done.11.refs_1_ = s16[144,512]{1,0:T(8,128)(2,1)S(1)} collective-permute-done((s16[144,512]{1,0:T(8,128)(2,1)S(1)}, s16[144,512]{1,0:T(8,128)(2,1)S(1)}, u32[]{:S(2)}, u32[]{:S(2)}) %collective-permute-start.11) | collective-permute-done | bytes 147488 | tf_op jit(solution)/shard_map/ppermute | solution.py:591
  61.6 3.5 %collective-permute-done.16.refs_3_ = s16[144,512]{1,0:T(8,128)(2,1)S(1)} collective-permute-done((s16[144,512]{1,0:T(8,128)(2,1)S(1)}, s16[144,512]{1,0:T(8,128)(2,1)S(1)}, u32[]{:S(2)}, u32[]{:S(2)}) %collective-permute-start.16) | collective-permute-done | bytes 147488 | tf_op jit(solution)/shard_map/ppermute | solution.py:591
  65.1 1.1 %total.3 = f32[128,512]{1,0:T(8,128)} custom-call(f32[128,512]{1,0:T(8,128)S(1)} %get-tuple-element.34.here_ref, s16[144,512]{1,0:T(8,128)(2,1)S(1)} %collective-permute-done.10.refs_0_, s16[144,512]{1,0:T(8,128)(2,1)S(1)} %collective-permute-done.11.refs_1_, s16[144,512]{1,0:T(8,128)(2,1)S(1)} %collective-permute-done.12.refs_2_, ...), custom_call_target="tpu_custom_call" | custom-call | tf_op jit(solution)/shard_map/total/pallas_call | solution.py:582
  (55 shorter events, 4.8 us)
Async XLA Ops:
  0.0 1.2 %copy-start = (f32[4,64,960]{2,1,0:T(8,128)S(1)}, f32[4,64,960]{2,1,0:T(8,128)}, u32[]{:S(2)}) copy-start(f32[4,64,960]{2,1,0:T(8,128)} %trace_ref.1) | copy-start | bytes 2949124
  1.2 22.7 %copy-start.1 = (f32[8,3840]{1,0:T(8,128)S(1)}, f32[8,3840]{1,0:T(8,128)}, u32[]{:S(2)}) copy-start(f32[8,3840]{1,0:T(8,128)} %constant.148.clone.refs_3_.refs_5_) | copy-start | bytes 368644
  1.5 14.1 %collective-permute-start = (s16[64,1024]{1,0:T(8,128)(2,1)S(1)}, s16[64,1024]{1,0:T(8,128)(2,1)S(1)}, u32[]{:S(2)}, u32[]{:S(2)}) collective-permute-start(s16[64,1024]{1,0:T(8,128)(2,1)S(1)} %get-tuple-element.26), channel_id=1, source_target_pairs={{0,16},{4,20},{8,24},{12,28},{16,0},{20,4},{24,8},{28,12},{1,17},{... | collective-permute-start | bytes 393224 | tf_op jit(solution)/shard_map/ppermute | solution.py:591
  5.6 10.0 %collective-permute-start.1 = (s16[64,1024]{1,0:T(8,128)(2,1)S(1)}, s16[64,1024]{1,0:T(8,128)(2,1)S(1)}, u32[]{:S(2)}, u32[]{:S(2)}) collective-permute-start(s16[64,1024]{1,0:T(8,128)(2,1)S(1)} %get-tuple-element.27), channel_id=1, source_target_pairs={{0,24},{4,28},{8,16},{12,20},{16,8},{20,12},{24,0},{28,4},{1,25},{... | collective-permute-start | bytes 393224 | tf_op jit(solution)/shard_map/ppermute | solution.py:591
  6.9 9.2 %collective-permute-start.2 = (s16[64,1024]{1,0:T(8,128)(2,1)S(1)}, s16[64,1024]{1,0:T(8,128)(2,1)S(1)}, u32[]{:S(2)}, u32[]{:S(2)}) collective-permute-start(s16[64,1024]{1,0:T(8,128)(2,1)S(1)} %get-tuple-element.28), channel_id=1, source_target_pairs={{0,8},{4,12},{8,0},{12,4},{16,24},{20,28},{24,16},{28,20},{1,9},{5... | collective-permute-start | bytes 393224 | tf_op jit(solution)/shard_map/ppermute | solution.py:591
  7.2 9.4 %collective-permute-start.6 = (s16[64,1024]{1,0:T(8,128)(2,1)S(1)}, s16[64,1024]{1,0:T(8,128)(2,1)S(1)}, u32[]{:S(2)}, u32[]{:S(2)}) collective-permute-start(s16[64,1024]{1,0:T(8,128)(2,1)S(1)} %get-tuple-element.29.refs_3_), channel_id=1, source_target_pairs={{0,4},{4,0},{8,12},{12,8},{16,20},{20,16},{24,28},{28,24},{1,5},{5... | collective-permute-start | bytes 393224 | tf_op jit(solution)/shard_map/ppermute | solution.py:591
  15.6 1.3 %collective-permute-start.3 = (s16[64,1024]{1,0:T(8,128)(2,1)S(1)}, s16[64,1024]{1,0:T(8,128)(2,1)S(1)}, u32[]{:S(2)}, u32[]{:S(2)}) collective-permute-start(s16[64,1024]{1,0:T(8,128)(2,1)S(1)} %collective-permute-done.refs_0_), channel_id=1, source_target_pairs={{0,4},{4,0},{8,12},{12,8},{16,20},{20,16},{24,28},{28,24},{1,5},{5... | collective-permute-start | bytes 393224 | tf_op jit(solution)/shard_map/ppermute | solution.py:591
  15.6 1.5 %collective-permute-start.4 = (s16[64,1024]{1,0:T(8,128)(2,1)S(1)}, s16[64,1024]{1,0:T(8,128)(2,1)S(1)}, u32[]{:S(2)}, u32[]{:S(2)}) collective-permute-start(s16[64,1024]{1,0:T(8,128)(2,1)S(1)} %collective-permute-done.1.refs_1_), channel_id=1, source_target_pairs={{0,4},{4,0},{8,12},{12,8},{16,20},{20,16},{24,28},{28,24},{1,5},{5... | collective-permute-start | bytes 393224 | tf_op jit(solution)/shard_map/ppermute | solution.py:591
  16.1 1.3 %collective-permute-start.5 = (s16[64,1024]{1,0:T(8,128)(2,1)S(1)}, s16[64,1024]{1,0:T(8,128)(2,1)S(1)}, u32[]{:S(2)}, u32[]{:S(2)}) collective-permute-start(s16[64,1024]{1,0:T(8,128)(2,1)S(1)} %collective-permute-done.2.refs_2_), channel_id=1, source_target_pairs={{0,4},{4,0},{8,12},{12,8},{16,20},{20,16},{24,28},{28,24},{1,5},{5... | collective-permute-start | bytes 393224 | tf_op jit(solution)/shard_map/ppermute | solution.py:591
  16.6 19.0 %copy-start.2 = (s32[64]{0:T(128)S(1)}, s32[64]{0:T(128)}, u32[]{:S(2)}) copy-start(s32[64]{0:T(128)} %param.8) | copy-start | bytes 772
  21.1 2.8 %collective-permute-start.8 = (bf16[32,7680]{1,0:T(8,128)(2,1)S(1)}, bf16[32,7680]{1,0:T(8,128)(2,1)S(1)}, u32[]{:S(2)}, u32[]{:S(2)}) collective-permute-start(bf16[32,7680]{1,0:T(8,128)(2,1)S(1)} %whiten.1.refs_0_.refs_1_.refs_2_), channel_id=1, source_target_pairs={{0,4},{4,0},{8,12},{12,8},{16,20},{20,16},{24,28},{28,24},{1,5},{5... | collective-permute-start | bytes 1474568 | tf_op jit(solution)/shard_map/ppermute | solution.py:591
  21.4 14.1 %collective-permute-start.7 = (bf16[32,7680]{1,0:T(8,128)(2,1)S(1)}, bf16[32,7680]{1,0:T(8,128)(2,1)S(1)}, u32[]{:S(2)}, u32[]{:S(2)}) collective-permute-start(bf16[32,7680]{1,0:T(8,128)(2,1)S(1)} %whiten.1.refs_0_.refs_1_.refs_2_), channel_id=1, source_target_pairs={{0,8},{4,12},{8,0},{12,4},{16,24},{20,28},{24,16},{28,20},{1,9},{5... | collective-permute-start | bytes 1474568 | tf_op jit(solution)/shard_map/ppermute | solution.py:591
  35.4 1.9 %collective-permute-start.9 = (bf16[32,7680]{1,0:T(8,128)(2,1)S(1)}, bf16[32,7680]{1,0:T(8,128)(2,1)S(1)}, u32[]{:S(2)}, u32[]{:S(2)}) collective-permute-start(bf16[32,7680]{1,0:T(8,128)(2,1)S(1)} %collective-permute-done.7.refs_3_), channel_id=1, source_target_pairs={{0,4},{4,0},{8,12},{12,8},{16,20},{20,16},{24,28},{28,24},{1,5},{5... | collective-permute-start | bytes 1474568 | tf_op jit(solution)/shard_map/ppermute | solution.py:591
  42.7 12.0 %collective-permute-start.13 = (s16[144,512]{1,0:T(8,128)(2,1)S(1)}, s16[144,512]{1,0:T(8,128)(2,1)S(1)}, u32[]{:S(2)}, u32[]{:S(2)}) collective-permute-start(s16[144,512]{1,0:T(8,128)(2,1)S(1)} %get-tuple-element.40), channel_id=1, source_target_pairs={{0,1},{1,0},{2,3},{3,2},{4,5},{5,4},{6,7},{7,6},{8,9},{9,8},{10,11... | collective-permute-start | bytes 442376 | tf_op jit(solution)/shard_map/ppermute | solution.py:591
  44.3 11.0 %collective-permute-start.14 = (s16[144,512]{1,0:T(8,128)(2,1)S(1)}, s16[144,512]{1,0:T(8,128)(2,1)S(1)}, u32[]{:S(2)}, u32[]{:S(2)}) collective-permute-start(s16[144,512]{1,0:T(8,128)(2,1)S(1)} %get-tuple-element.41), channel_id=1, source_target_pairs={{0,2},{1,3},{2,0},{3,1},{4,6},{5,7},{6,4},{7,5},{8,10},{9,11},{10,... | collective-permute-start | bytes 442376 | tf_op jit(solution)/shard_map/ppermute | solution.py:591
  45.8 9.5 %collective-permute-start.15 = (s16[144,512]{1,0:T(8,128)(2,1)S(1)}, s16[144,512]{1,0:T(8,128)(2,1)S(1)}, u32[]{:S(2)}, u32[]{:S(2)}) collective-permute-start(s16[144,512]{1,0:T(8,128)(2,1)S(1)} %get-tuple-element.42), channel_id=1, source_target_pairs={{0,3},{1,2},{2,1},{3,0},{4,7},{5,6},{6,5},{7,4},{8,11},{9,10},{10,... | collective-permute-start | bytes 442376 | tf_op jit(solution)/shard_map/ppermute | solution.py:591
  51.7 8.3 %collective-permute-start.10 = (s16[144,512]{1,0:T(8,128)(2,1)S(1)}, s16[144,512]{1,0:T(8,128)(2,1)S(1)}, u32[]{:S(2)}, u32[]{:S(2)}) collective-permute-start(s16[144,512]{1,0:T(8,128)(2,1)S(1)} %get-tuple-element.35), channel_id=1, source_target_pairs={{0,1},{1,0},{2,3},{3,2},{4,5},{5,4},{6,7},{7,6},{8,9},{9,8},{10,11... | collective-permute-start | bytes 442376 | tf_op jit(solution)/shard_map/ppermute | solution.py:591
  53.2 8.3 %collective-permute-start.11 = (s16[144,512]{1,0:T(8,128)(2,1)S(1)}, s16[144,512]{1,0:T(8,128)(2,1)S(1)}, u32[]{:S(2)}, u32[]{:S(2)}) collective-permute-start(s16[144,512]{1,0:T(8,128)(2,1)S(1)} %get-tuple-element.36), channel_id=1, source_target_pairs={{0,2},{1,3},{2,0},{3,1},{4,6},{5,7},{6,4},{7,5},{8,10},{9,11},{10,... | collective-permute-start | bytes 442376 | tf_op jit(solution)/shard_map/ppermute | solution.py:591
  54.8 6.8 %collective-permute-start.12 = (s16[144,512]{1,0:T(8,128)(2,1)S(1)}, s16[144,512]{1,0:T(8,128)(2,1)S(1)}, u32[]{:S(2)}, u32[]{:S(2)}) collective-permute-start(s16[144,512]{1,0:T(8,128)(2,1)S(1)} %get-tuple-element.37), channel_id=1, source_target_pairs={{0,3},{1,2},{2,1},{3,0},{4,7},{5,6},{6,5},{7,4},{8,11},{9,10},{10,... | collective-permute-start | bytes 442376 | tf_op jit(solution)/shard_map/ppermute | solution.py:591
  55.7 9.3 %collective-permute-start.16 = (s16[144,512]{1,0:T(8,128)(2,1)S(1)}, s16[144,512]{1,0:T(8,128)(2,1)S(1)}, u32[]{:S(2)}, u32[]{:S(2)}) collective-permute-start(s16[144,512]{1,0:T(8,128)(2,1)S(1)} %total.2), channel_id=1, source_target_pairs={{0,16},{4,20},{8,24},{12,28},{16,0},{20,4},{24,8},{28,12},{1,17},{... | collective-permute-start | bytes 442376 | tf_op jit(solution)/shard_map/ppermute | solution.py:591
